TPU v7x, 32 devices: a whole 2x2x4 slice. The times are simulated.
32 devices in a mesh: prompt: 4 (over x, core), branch: 8 (over z, y).
Axes of the slice: x: 2, y: 2, z: 4, core: 2. Of those that a mesh axis runs over, the one named last changes fastest.
Arguments:
- query: bfloat16 [32, 512, 2048], P(('prompt', 'branch')), may hold values from -6 to 6
- branch_kv: bfloat16 [32, 512, 2, 1024], P(('prompt', 'branch'))
- prefix_kv: bfloat16 [128, 2, 1024], P(('prompt', 'branch'))
- cotangent: bfloat16 [32, 512, 2048], P(('prompt', 'branch')), may hold values from -48 to 48
- subtree_end: int32 [32, 512], P(('prompt', 'branch')), may hold values from 1 to 512, as said below
- lengths: int32 [32], P(('prompt', 'branch')), may hold values from 1 to 512, as said below
Outputs:
- attended: bfloat16 [32, 512, 2048], P(('prompt', 'branch'))
- query_grad: bfloat16 [32, 512, 2048], P(('prompt', 'branch'))
- branch_kv_grad: bfloat16 [32, 512, 2, 1024], P(('prompt', 'branch'))
- prefix_kv_grad: bfloat16 [128, 2, 1024], P(('prompt', 'branch'))
Inputs may be any that keep to these rules, and one draw needn't show every extreme that they name: The positions of each branch are in depth-first order of a token tree rooted at position 0; subtree_end[b, t] is one past the last position of the subtree under t, so it exceeds t, and the root's value is 512. Positions from lengths[b] on are padding; some branch has all 512 positions live.
All inputs are finite; a program needn't handle non-finite values.
Results may differ from a plain program's by a relative error of at most 0.0071.
Values may be sent and summed in bfloat16 or wider, within the bound.
A program may use at most 128 MiB of HBM per device.

v0:
```python
import jax
import jax.numpy as jnp
from jax import lax
from jax.sharding import PartitionSpec as P

QUERY_HEADS = 16
KEY_VALUE_HEADS = 8
HEAD_SIZE = 128


softcap = 50.0
query_scale = 144.0 ** (-0.5)


def scores_for(queries, key_rows, visible):
    raw = jnp.einsum("qrd,nd->rqn", queries, key_rows, preferred_element_type=jnp.float32)
    capped = softcap * jnp.tanh(raw * query_scale / softcap)
    weights = jnp.where(visible[None], jnp.exp(capped), 0.0)
    return (capped, weights)


def collect_prefix(prefix_kv):
    return lax.all_gather(prefix_kv, ("prompt", "branch"), axis=0, tiled=True)


def return_prefix(term):
    return lax.psum_scatter(term, ("prompt", "branch"), scatter_dimension=0, tiled=True)


def body(query, branch_kv, prefix_kv, cotangent, subtree_end, lengths):
    query_group_ratio = QUERY_HEADS // KEY_VALUE_HEADS
    rows = query.shape[1]
    positions = jnp.arange(rows, dtype=jnp.int32)
    live = positions < lengths[0]
    prefix_all = collect_prefix(prefix_kv)
    prefix_rows = prefix_all.shape[0]
    ends = subtree_end[0]
    tree = (positions[None, :] <= positions[:, None]) & (positions[:, None] < ends[None, :])
    visible = jnp.concatenate([jnp.ones((rows, prefix_rows), dtype=bool), tree], axis=1)
    queries = query[0].reshape(rows, QUERY_HEADS, HEAD_SIZE)
    keys_all = jnp.concatenate([prefix_all, branch_kv[0]], axis=0)
    overall_rows = keys_all.shape[0]
    group_index = jnp.arange(KEY_VALUE_HEADS, dtype=jnp.int32)

    def forward_group(index):
        q_g = lax.dynamic_slice_in_dim(queries, index * query_group_ratio, query_group_ratio, 1)
        kv_g = lax.dynamic_slice_in_dim(keys_all, index * HEAD_SIZE, HEAD_SIZE, 2)
        capped, weights = scores_for(q_g, kv_g[:, 0], visible)
        total = jnp.sum(weights, axis=-1)
        probs = (weights / total[..., None]).astype(jnp.bfloat16)
        context = jnp.einsum("rqn,nd->qrd", probs, kv_g[:, 1], preferred_element_type=jnp.float32)
        return (context, total)

    context_outputs, totals = lax.map(forward_group, group_index)
    context_rows = jnp.transpose(context_outputs, (1, 0, 2, 3)).reshape(
        rows, QUERY_HEADS * HEAD_SIZE
    )
    attended = jnp.where(live[:, None], context_rows, 0.0).astype(jnp.bfloat16)
    prefix_back = lax.all_gather(prefix_kv, ("prompt", "branch"), axis=0, tiled=True)
    keys_back = jnp.concatenate([prefix_back, branch_kv[0]], axis=0)
    grad_out = jnp.where(live[:, None], cotangent[0], jnp.zeros_like(cotangent[0])).reshape(
        rows, QUERY_HEADS, HEAD_SIZE
    )

    def backward_group(items):
        index, context, total = items
        q_g = lax.dynamic_slice_in_dim(queries, index * query_group_ratio, query_group_ratio, 1)
        g_g = lax.dynamic_slice_in_dim(grad_out, index * query_group_ratio, query_group_ratio, 1)
        kv_g = lax.dynamic_slice_in_dim(keys_back, index * HEAD_SIZE, HEAD_SIZE, 2)
        capped, weights = scores_for(q_g, kv_g[:, 0], visible)
        probs = weights / total[..., None]
        probs_b = probs.astype(jnp.bfloat16)
        grad_prob = jnp.einsum("qrd,nd->rqn", g_g, kv_g[:, 1], preferred_element_type=jnp.float32)
        delta = jnp.transpose(jnp.sum(g_g.astype(jnp.float32) * context, axis=-1))
        score_grad = (
            probs * (grad_prob - delta[..., None]) * (1.0 - (capped / softcap) ** 2) * query_scale
        ).astype(jnp.bfloat16)
        dquery = jnp.einsum(
            "rqn,nd->qrd", score_grad, kv_g[:, 0], preferred_element_type=jnp.float32
        )
        dkey = jnp.einsum("rqn,qrd->nd", score_grad, q_g, preferred_element_type=jnp.float32)
        dvalue = jnp.einsum("rqn,qrd->nd", probs_b, g_g, preferred_element_type=jnp.float32)
        return (dquery, jnp.stack([dkey, dvalue], axis=1))

    query_gradients, key_value_gradients = lax.map(
        backward_group, (group_index, context_outputs, totals)
    )
    query_grad = (
        jnp.transpose(query_gradients, (1, 0, 2, 3))
        .reshape(rows, QUERY_HEADS * HEAD_SIZE)
        .astype(jnp.bfloat16)
    )
    summed_key_values = jnp.transpose(key_value_gradients, (1, 2, 0, 3)).reshape(
        overall_rows, 2, KEY_VALUE_HEADS * HEAD_SIZE
    )
    prefix_kv_grad = return_prefix(summed_key_values[:prefix_rows]).astype(jnp.bfloat16)
    branch_kv_grad = summed_key_values[prefix_rows:].astype(jnp.bfloat16)
    return (attended[None], query_grad[None], branch_kv_grad[None], prefix_kv_grad)


def solution(mesh):
    in_specs = (
        P(("prompt", "branch"), None, None),
        P(("prompt", "branch"), None, None, None),
        P(("prompt", "branch"), None, None),
        P(("prompt", "branch"), None, None),
        P(("prompt", "branch"), None),
        P(("prompt", "branch")),
    )
    out_specs = (
        P(("prompt", "branch"), None, None),
        P(("prompt", "branch"), None, None),
        P(("prompt", "branch"), None, None, None),
        P(("prompt", "branch"), None, None),
    )
    return jax.shard_map(body, mesh=mesh, in_specs=in_specs, out_specs=out_specs, check_vma=False)
```

profile of v0, /device:TPU:0, one launch (start us, length us, event | category | flops | bytes accessed | tf_op | source)
XLA Modules:
  0.0 370.7 jit_solution(2222386605066740789)
XLA Ops:
  2.9 72.7 %all_gather.4 = bf16[128,2,1024]{2,1,0:T(2,128)(2,1)S(1)} all-gather(bf16[4,2,1024]{2,1,0:T(2,128)(2,1)S(1)} %copy-done.7), channel_id=1, replica_groups=mesh['prompt'=4,'branch'=8] {'prompt','branch'}, dimensions={0}, use_global_device_ids=true | all-gather | bytes 540672 | tf_op jit(solution)/shard_map/all_gather | solution.py:23
  84.0 71.8 %while.30 = (s32[]{:T(128)}, f32[8,512,2,128]{1,3,2,0:T(8,128)}, f32[8,2,512]{2,1,0:T(2,128)S(1)}, s32[8]{0:T(128)S(1)}, bf16[640,2,1024]{2,0,1:T(8,128)(2,1)}, ...) while((s32[]{:T(128)}, f32[8,512,2,128]{1,3,2,0:T(8,128)}, ...), condition=%wide.region_2.3_spmd.clone, body=%wide.region_0.2_spmd.sunk.clone | while | flops 341441536 | bytes 7029477 | solution.py:54
  85.9 3.3 fusion.69
  89.2 3.7 %fusion.70 = f32[8,512,2,128]{1,3,2,0:T(8,128)} fusion(f32[8,512,2,128]{1,3,2,0:T(8,128)} %get-tuple-element.483, s32[]{:T(128)} %get-tuple-element.482, f32[640,512,2]{1,0,2:T(8,128)} %get-tuple-element.423, f32[2,512]{1,0:T(2,128)S(1)} %get-tuple-element.424, pred[512,640]{0,1:T(8,128)(4,1)S(1)} %get-tuple-element.496, ...), kind=kOutput, calls=%fused_computation.5.clone.1.clone | convolution fusion | flops 171048960 | bytes 3641864 | tf_op jit(solution)/shard_map/while/body/eval_jaxpr/rqn,nd->qrd/dot_general | solution.py:51
  94.9 3.3 fusion.69
  98.2 3.7 %fusion.70 = f32[8,512,2,128]{1,3,2,0:T(8,128)} fusion(f32[8,512,2,128]{1,3,2,0:T(8,128)} %get-tuple-element.483, s32[]{:T(128)} %get-tuple-element.482, f32[640,512,2]{1,0,2:T(8,128)} %get-tuple-element.423, f32[2,512]{1,0:T(2,128)S(1)} %get-tuple-element.424, pred[512,640]{0,1:T(8,128)(4,1)S(1)} %get-tuple-element.496, ...), kind=kOutput, calls=%fused_computation.5.clone.1.clone | convolution fusion | flops 171048960 | bytes 3641864 | tf_op jit(solution)/shard_map/while/body/eval_jaxpr/rqn,nd->qrd/dot_general | solution.py:51
  103.8 3.3 fusion.69
  107.2 3.7 %fusion.70 = f32[8,512,2,128]{1,3,2,0:T(8,128)} fusion(f32[8,512,2,128]{1,3,2,0:T(8,128)} %get-tuple-element.483, s32[]{:T(128)} %get-tuple-element.482, f32[640,512,2]{1,0,2:T(8,128)} %get-tuple-element.423, f32[2,512]{1,0:T(2,128)S(1)} %get-tuple-element.424, pred[512,640]{0,1:T(8,128)(4,1)S(1)} %get-tuple-element.496, ...), kind=kOutput, calls=%fused_computation.5.clone.1.clone | convolution fusion | flops 171048960 | bytes 3641864 | tf_op jit(solution)/shard_map/while/body/eval_jaxpr/rqn,nd->qrd/dot_general | solution.py:51
  112.8 3.3 fusion.69
  116.1 3.7 %fusion.70 = f32[8,512,2,128]{1,3,2,0:T(8,128)} fusion(f32[8,512,2,128]{1,3,2,0:T(8,128)} %get-tuple-element.483, s32[]{:T(128)} %get-tuple-element.482, f32[640,512,2]{1,0,2:T(8,128)} %get-tuple-element.423, f32[2,512]{1,0:T(2,128)S(1)} %get-tuple-element.424, pred[512,640]{0,1:T(8,128)(4,1)S(1)} %get-tuple-element.496, ...), kind=kOutput, calls=%fused_computation.5.clone.1.clone | convolution fusion | flops 171048960 | bytes 3641864 | tf_op jit(solution)/shard_map/while/body/eval_jaxpr/rqn,nd->qrd/dot_general | solution.py:51
  121.7 3.3 fusion.69
  125.1 3.7 %fusion.70 = f32[8,512,2,128]{1,3,2,0:T(8,128)} fusion(f32[8,512,2,128]{1,3,2,0:T(8,128)} %get-tuple-element.483, s32[]{:T(128)} %get-tuple-element.482, f32[640,512,2]{1,0,2:T(8,128)} %get-tuple-element.423, f32[2,512]{1,0:T(2,128)S(1)} %get-tuple-element.424, pred[512,640]{0,1:T(8,128)(4,1)S(1)} %get-tuple-element.496, ...), kind=kOutput, calls=%fused_computation.5.clone.1.clone | convolution fusion | flops 171048960 | bytes 3641864 | tf_op jit(solution)/shard_map/while/body/eval_jaxpr/rqn,nd->qrd/dot_general | solution.py:51
  130.7 3.3 fusion.69
  134.0 3.8 %fusion.70 = f32[8,512,2,128]{1,3,2,0:T(8,128)} fusion(f32[8,512,2,128]{1,3,2,0:T(8,128)} %get-tuple-element.483, s32[]{:T(128)} %get-tuple-element.482, f32[640,512,2]{1,0,2:T(8,128)} %get-tuple-element.423, f32[2,512]{1,0:T(2,128)S(1)} %get-tuple-element.424, pred[512,640]{0,1:T(8,128)(4,1)S(1)} %get-tuple-element.496, ...), kind=kOutput, calls=%fused_computation.5.clone.1.clone | convolution fusion | flops 171048960 | bytes 3641864 | tf_op jit(solution)/shard_map/while/body/eval_jaxpr/rqn,nd->qrd/dot_general | solution.py:51
  139.7 3.3 fusion.69
  143.0 3.8 %fusion.70 = f32[8,512,2,128]{1,3,2,0:T(8,128)} fusion(f32[8,512,2,128]{1,3,2,0:T(8,128)} %get-tuple-element.483, s32[]{:T(128)} %get-tuple-element.482, f32[640,512,2]{1,0,2:T(8,128)} %get-tuple-element.423, f32[2,512]{1,0:T(2,128)S(1)} %get-tuple-element.424, pred[512,640]{0,1:T(8,128)(4,1)S(1)} %get-tuple-element.496, ...), kind=kOutput, calls=%fused_computation.5.clone.1.clone | convolution fusion | flops 171048960 | bytes 3641864 | tf_op jit(solution)/shard_map/while/body/eval_jaxpr/rqn,nd->qrd/dot_general | solution.py:51
  148.7 3.3 fusion.69
  152.0 3.8 %fusion.70 = f32[8,512,2,128]{1,3,2,0:T(8,128)} fusion(f32[8,512,2,128]{1,3,2,0:T(8,128)} %get-tuple-element.483, s32[]{:T(128)} %get-tuple-element.482, f32[640,512,2]{1,0,2:T(8,128)} %get-tuple-element.423, f32[2,512]{1,0:T(2,128)S(1)} %get-tuple-element.424, pred[512,640]{0,1:T(8,128)(4,1)S(1)} %get-tuple-element.496, ...), kind=kOutput, calls=%fused_computation.5.clone.1.clone | convolution fusion | flops 171048960 | bytes 3641864 | tf_op jit(solution)/shard_map/while/body/eval_jaxpr/rqn,nd->qrd/dot_general | solution.py:51
  156.4 3.9 %copy.46 = bf16[1,512,2048]{1,2,0:T(8,128)(2,1)} copy(bf16[1,512,2048]{2,1,0:T(8,128)(2,1)} %param.13) | data formatting | bytes 4194304 | tf_op args[3]
  160.4 3.0 broadcast_select_fusion
  164.9 139.3 %while.31 = (s32[]{:T(128)}, bf16[8,512,2,128]{1,3,2,0:T(8,128)(2,1)}, f32[8,640,2,128]{3,1,2,0:T(8,128)}, s32[8]{0:T(128)S(1)}, bf16[640,2,1024]{2,0,1:T(8,128)...) while((s32[]{:T(128)}, ...), condition=%wide.region_5.6_spmd.clone, body=%wide.region_3.5_spmd.sunk.clone | while | flops 849902592 | bytes 41936308 | solution.py:85
  312.7 48.3 %all-reduce.3 = bf16[128,2,1024]{2,1,0:T(2,128)(2,1)S(1)} all-reduce(f32[128,2,1024]{2,1,0:T(2,128)S(1)} %slice.38), channel_id=2, replica_groups=mesh['prompt'=4,'branch'=8] {'prompt','branch'}, use_global_device_ids=true, to_apply=%region_6.7.clone | all-reduce | flops 262144 | bytes 1572864
  361.6 3.9 %copy.60 = bf16[1,512,2048]{2,1,0:T(8,128)(2,1)} copy(bf16[1,512,2048]{1,2,0:T(8,128)(2,1)} %bitcast.38) | data formatting | bytes 4194304 | tf_op jit(solution)/shard_map/convert_element_type | solution.py:91
  365.5 3.4 copy.59
  (244 shorter events, 156.9 us)
Async XLA Ops:
  80.7 3.1 copy-start.8
  173.4 4.1 %copy-start.1 = (bf16[512,2,128]{0,2,1:T(8,128)(2,1)S(1)}, bf16[512,2,128]{0,2,1:T(8,128)(2,1)}, u32[]{:S(2)}) copy-start(bf16[512,2,128]{0,2,1:T(8,128)(2,1)} %copy-done) | copy-start | bytes 786436 | tf_op jit(solution)/shard_map/while
  179.4 3.0 copy-start.3
  179.4 3.0 copy-start.6
  190.8 4.1 %copy-start.1 = (bf16[512,2,128]{0,2,1:T(8,128)(2,1)S(1)}, bf16[512,2,128]{0,2,1:T(8,128)(2,1)}, u32[]{:S(2)}) copy-start(bf16[512,2,128]{0,2,1:T(8,128)(2,1)} %copy-done) | copy-start | bytes 786436 | tf_op jit(solution)/shard_map/while
  196.8 3.0 copy-start.3
  196.8 3.0 copy-start.6
  208.2 4.1 %copy-start.1 = (bf16[512,2,128]{0,2,1:T(8,128)(2,1)S(1)}, bf16[512,2,128]{0,2,1:T(8,128)(2,1)}, u32[]{:S(2)}) copy-start(bf16[512,2,128]{0,2,1:T(8,128)(2,1)} %copy-done) | copy-start | bytes 786436 | tf_op jit(solution)/shard_map/while
  214.2 3.0 copy-start.3
  214.2 3.0 copy-start.6
  225.6 4.1 %copy-start.1 = (bf16[512,2,128]{0,2,1:T(8,128)(2,1)S(1)}, bf16[512,2,128]{0,2,1:T(8,128)(2,1)}, u32[]{:S(2)}) copy-start(bf16[512,2,128]{0,2,1:T(8,128)(2,1)} %copy-done) | copy-start | bytes 786436 | tf_op jit(solution)/shard_map/while
  231.6 3.0 copy-start.3
  231.6 3.0 copy-start.6
  243.0 4.1 %copy-start.1 = (bf16[512,2,128]{0,2,1:T(8,128)(2,1)S(1)}, bf16[512,2,128]{0,2,1:T(8,128)(2,1)}, u32[]{:S(2)}) copy-start(bf16[512,2,128]{0,2,1:T(8,128)(2,1)} %copy-done) | copy-start | bytes 786436 | tf_op jit(solution)/shard_map/while
  249.0 3.0 copy-start.3
  249.0 3.0 copy-start.6
  260.4 4.1 %copy-start.1 = (bf16[512,2,128]{0,2,1:T(8,128)(2,1)S(1)}, bf16[512,2,128]{0,2,1:T(8,128)(2,1)}, u32[]{:S(2)}) copy-start(bf16[512,2,128]{0,2,1:T(8,128)(2,1)} %copy-done) | copy-start | bytes 786436 | tf_op jit(solution)/shard_map/while
  266.4 3.0 copy-start.3
  266.4 3.0 copy-start.6
  277.9 4.1 %copy-start.1 = (bf16[512,2,128]{0,2,1:T(8,128)(2,1)S(1)}, bf16[512,2,128]{0,2,1:T(8,128)(2,1)}, u32[]{:S(2)}) copy-start(bf16[512,2,128]{0,2,1:T(8,128)(2,1)} %copy-done) | copy-start | bytes 786436 | tf_op jit(solution)/shard_map/while
  283.9 3.0 copy-start.3
  283.9 3.0 copy-start.6
  295.3 4.1 %copy-start.1 = (bf16[512,2,128]{0,2,1:T(8,128)(2,1)S(1)}, bf16[512,2,128]{0,2,1:T(8,128)(2,1)}, u32[]{:S(2)}) copy-start(bf16[512,2,128]{0,2,1:T(8,128)(2,1)} %copy-done) | copy-start | bytes 786436 | tf_op jit(solution)/shard_map/while
  301.3 3.0 copy-start.3
  (27 other events, 42.5 us)
where the time goes:
time: 374 us; the launch traced here: 371 us
  matrix products  133 us (36%)
  blocking collectives  121 us (32%)
  local copies, waits for them, and re-layouts  77.4 us (21%)
  loops' own time  20.5 us (5%)
  other arithmetic  17.1 us (5%)
    all_gather x1, blocking collectives, collect_prefix(): return lax.all_gather(prefix_kv, ('prompt', 'branch'), axis=0, tiled=True)  72.7 us
    unnamed x1, blocking collectives  48.3 us
    dot_general x16, matrix products, scores_for(): jnp.einsum('qrd,nd->rqn', queries, key_rows, preferred_element_type=jnp.f...  39 us
    dot_general x8, matrix products, forward_group(): jnp.einsum('rqn,nd->qrd', probs, kv_g[:, 1], preferred_element_type=jnp.f...  29.9 us
    dynamic_slice x16, local copies, waits for them, and re-layouts, body(): lax.map(backward_group, (group_index, context_outputs, totals))  24.8 us
    dot_general x8, matrix products, backward_group(): jnp.einsum('qrd,nd->rqn', g_g, kv_g[:, 1], preferred_element_type=jnp.flo...  21.2 us
    dot_general x8, matrix products, backward_group(): jnp.einsum('rqn,nd->qrd', score_grad, kv_g[:, 0], preferred_element_type=...  16.6 us
    dot_general x8, matrix products, backward_group(): jnp.einsum('rqn,qrd->nd', probs_b, g_g, preferred_element_type=jnp.float32)  14.8 us

commit v1 on v0

v1 whole, which is shorter than its diff:
```python
import functools

import jax
import jax.numpy as jnp
from jax import lax
from jax.experimental import pallas as pl
from jax.experimental.pallas import tpu as pltpu
from jax.sharding import PartitionSpec as P

QUERY_HEADS = 16
KEY_VALUE_HEADS = 8
HEAD_SIZE = 128
RATIO = QUERY_HEADS // KEY_VALUE_HEADS

softcap = 50.0
query_scale = 144.0 ** (-0.5)
MESH = pl.DeviceIdType.MESH
QB = 256
KC = 128


def nt(a, b):
    return lax.dot_general(a, b, (((1,), (1,)), ((), ())), preferred_element_type=jnp.float32)


def nn(a, b):
    return jnp.dot(a, b, preferred_element_type=jnp.float32)


def greet(peers):
    barrier = pltpu.get_barrier_semaphore()
    for peer in peers:
        pl.semaphore_signal(barrier, inc=1, device_id=peer, device_id_type=MESH)
    pl.semaphore_wait(barrier, len(peers))


def exchange_peers(n_p, n_b):
    p, b = lax.axis_index("prompt"), lax.axis_index("branch")
    ring = [(p, lax.rem(b + k, n_b)) for k in range(1, n_b)]
    pairs = []
    step = 1
    while step < n_p:
        low = lax.rem(lax.div(p, step), 2)
        pairs.append((p + step - 2 * step * low, b))
        step *= 2
    return p, b, ring, pairs


def gather_kernel(n_p, n_b, src, out, send_b, recv_b, send_p, recv_p, own_sem):
    rows = src.shape[0]
    p, b, ring, pairs = exchange_peers(n_p, n_b)
    greet(ring + pairs)
    mine = out.at[pl.ds((p * n_b + b) * rows, rows)]
    local = pltpu.make_async_copy(src, mine, own_sem)
    local.start()
    copies = []
    for k, peer in enumerate(ring):
        copy = pltpu.make_async_remote_copy(
            src_ref=src, dst_ref=mine, send_sem=send_b.at[k], recv_sem=recv_b.at[k],
            device_id=peer, device_id_type=MESH)
        copy.start()
        copies.append(copy)
    local.wait()
    for copy in copies:
        copy.wait()
    step = 1
    for k, peer in enumerate(pairs):
        first = lax.div(p, step) * step
        part = out.at[pl.ds(first * n_b * rows, step * n_b * rows)]
        copy = pltpu.make_async_remote_copy(
            src_ref=part, dst_ref=part, send_sem=send_p.at[k], recv_sem=recv_p.at[k],
            device_id=peer, device_id_type=MESH)
        copy.start()
        copy.wait()
        step *= 2


def gather_prefix(n_p, n_b, prefix_kv):
    rows = prefix_kv.shape[0]
    n_k = max(n_p.bit_length() - 1, 1)
    return pl.pallas_call(
        functools.partial(gather_kernel, n_p, n_b),
        out_shape=jax.ShapeDtypeStruct((rows * n_p * n_b,) + prefix_kv.shape[1:], prefix_kv.dtype),
        in_specs=[pl.BlockSpec(memory_space=pl.ANY)],
        out_specs=pl.BlockSpec(memory_space=pl.ANY),
        scratch_shapes=[
            pltpu.SemaphoreType.DMA((n_b,)),
            pltpu.SemaphoreType.DMA((n_b,)),
            pltpu.SemaphoreType.DMA((n_k,)),
            pltpu.SemaphoreType.DMA((n_k,)),
            pltpu.SemaphoreType.DMA,
        ],
        compiler_params=pltpu.CompilerParams(collective_id=0, has_side_effects=True),
        name="gather_prefix",
    )(prefix_kv)


def scatter_kernel(n_p, n_b, term, out, work, land_p, land_b, send_p, recv_p, send_b, recv_b):
    p, b, ring, pairs = exchange_peers(n_p, n_b)
    greet(ring + pairs)
    src = term
    step = n_p // 2
    first = 0
    at = 0
    for k in range(len(pairs)):
        pass
    width = n_p
    parts = list(range(n_p))
    step = 1
    level = 0
    while step < n_p:
        peer = pairs[level]
        bit = lax.rem(lax.div(p, step), 2)
        half = n_p // (2 * step)
        copies = []
        low = lax.rem(p, step)
        for i in range(half):
            theirs = low + (1 - bit) * step + i * 2 * step
            source = src.at[pl.ds(theirs * n_b, n_b)]
            copy = pltpu.make_async_remote_copy(
                src_ref=source, dst_ref=land_p.at[pl.ds((at + i) * n_b, n_b)],
                send_sem=send_p.at[at + i], recv_sem=recv_p.at[at + i],
                device_id=peer, device_id_type=MESH)
            copy.start()
            copies.append(copy)
        for copy in copies:
            copy.wait()
        for i in range(half):
            ours = low + bit * step + i * 2 * step
            own = src[pl.ds(ours * n_b, n_b)].astype(jnp.float32)
            got = land_p[pl.ds((at + i) * n_b, n_b)].astype(jnp.float32)
            work[pl.ds(ours * n_b, n_b)] = (own + got).astype(work.dtype)
        src = work
        at += half
        step *= 2
        level += 1
    copies = []
    for k, (_, other) in enumerate(ring):
        copy = pltpu.make_async_remote_copy(
            src_ref=src.at[p * n_b + other], dst_ref=land_b.at[k],
            send_sem=send_b.at[k], recv_sem=recv_b.at[k],
            device_id=(p, other), device_id_type=MESH)
        copy.start()
        copies.append(copy)
    total = src[p * n_b + b].astype(jnp.float32)
    for copy in copies:
        copy.wait()
    for k in range(len(ring)):
        total += land_b[k].astype(jnp.float32)
    out[...] = total.astype(out.dtype)


def scatter_prefix(n_p, n_b, term):
    blocks, high, wide = term.shape
    n_k = max(n_p - 1, 1)
    return pl.pallas_call(
        functools.partial(scatter_kernel, n_p, n_b),
        out_shape=jax.ShapeDtypeStruct((high, wide), jnp.bfloat16),
        in_specs=[pl.BlockSpec(memory_space=pltpu.VMEM)],
        out_specs=pl.BlockSpec(memory_space=pltpu.VMEM),
        scratch_shapes=[
            pltpu.VMEM((blocks, high, wide), term.dtype),
            pltpu.VMEM((n_k * n_b, high, wide), term.dtype),
            pltpu.VMEM((n_b, high, wide), term.dtype),
            pltpu.SemaphoreType.DMA((n_k,)),
            pltpu.SemaphoreType.DMA((n_k,)),
            pltpu.SemaphoreType.DMA((n_b,)),
            pltpu.SemaphoreType.DMA((n_b,)),
        ],
        compiler_params=pltpu.CompilerParams(collective_id=1, has_side_effects=True,
                                             vmem_limit_bytes=24 * 1024 * 1024),
        name="scatter_prefix",
    )(term)


def attention_kernel(lens, ends, q_ref, g_ref, kv_ref, pkv_ref, att, qg, kvg, pg,
                     mask, k_all, v_all, kt, vt, p_s, t_s, ds_s):
    rows = q_ref.shape[0]
    prefix = pkv_ref.shape[1]
    length = lens[0]

    @pl.when(pl.program_id(0) == 0)
    def _():
        for r in range(0, rows, KC):
            span = jnp.broadcast_to(ends[:, r:r + KC].astype(jnp.float32), (KC, KC))
            stop = jnp.transpose(span)[:, :1]
            t = lax.broadcasted_iota(jnp.int32, (KC, rows), 0) + r
            i = lax.broadcasted_iota(jnp.int32, (KC, rows), 1)
            seen = (t <= i) & (i.astype(jnp.float32) < stop)
            mask[r:r + KC, :] = jnp.where(seen, 1.0, 0.0)

    k_all[:prefix] = pkv_ref[0]
    k_all[prefix:] = kv_ref[0]
    v_all[:prefix] = pkv_ref[1]
    v_all[prefix:] = kv_ref[1]
    kt[...] = jnp.transpose(k_all[...])
    vt[...] = jnp.transpose(v_all[...])

    dk = [None] * ((prefix + rows) // KC)
    dv = [None] * ((prefix + rows) // KC)
    for h in range(RATIO):
        cols = slice(h * HEAD_SIZE, (h + 1) * HEAD_SIZE)
        for j in range(rows // QB):
            spot = slice(j * QB, (j + 1) * QB)
            n = prefix + (j + 1) * QB
            chunks = n // KC
            live = lax.broadcasted_iota(jnp.int32, (QB, HEAD_SIZE), 0) + j * QB < length
            q = q_ref[spot, cols]
            g = jnp.where(live, g_ref[spot, cols], jnp.zeros((), jnp.bfloat16))
            total = jnp.zeros((1, QB), jnp.float32)
            for c in range(chunks):
                at = slice(c * KC, (c + 1) * KC)
                t = jnp.tanh(nt(k_all[at], q) * (query_scale / softcap))
                w = jnp.exp(softcap * t)
                if c * KC >= prefix:
                    w = w * mask[c * KC - prefix:(c + 1) * KC - prefix, spot]
                total += jnp.sum(w, axis=0, keepdims=True)
                p_s[at] = w
                t_s[at] = t
            inverse = 1.0 / total
            probs = []
            for c in range(chunks):
                at = slice(c * KC, (c + 1) * KC)
                p = p_s[at] * inverse
                p_s[at] = p
                probs.append(p.astype(jnp.bfloat16))
            probs = jnp.concatenate(probs, axis=0)
            context = nn(vt[:, :n], probs)
            delta = jnp.sum(jnp.transpose(g).astype(jnp.float32) * context, axis=0, keepdims=True)
            att[spot, cols] = jnp.where(
                live, jnp.transpose(context.astype(jnp.bfloat16)), jnp.zeros((), jnp.bfloat16))
            for c in range(chunks):
                at = slice(c * KC, (c + 1) * KC)
                t = t_s[at]
                score = p_s[at] * (nt(v_all[at], g) - delta) * (1.0 - t * t)
                ds_s[at] = score.astype(jnp.bfloat16)
            scores = ds_s[:n]
            dq = nn(kt[:, :n], scores) * query_scale
            qg[spot, cols] = jnp.transpose(dq.astype(jnp.bfloat16))
            for c in range(chunks):
                at = slice(c * KC, (c + 1) * KC)
                one = nn(scores[at], q)
                two = nn(probs[at], g)
                dk[c] = one if dk[c] is None else dk[c] + one
                dv[c] = two if dv[c] is None else dv[c] + two
    for c in range(len(dk)):
        if c * KC < prefix:
            pg[0, c * KC:(c + 1) * KC] = dk[c] * query_scale
            pg[1, c * KC:(c + 1) * KC] = dv[c]
        else:
            at = slice(c * KC - prefix, (c + 1) * KC - prefix)
            kvg[0, at] = (dk[c] * query_scale).astype(jnp.bfloat16)
            kvg[1, at] = dv[c].astype(jnp.bfloat16)


def attention(lengths, ends, query, cotangent, kv, pkv):
    rows, wide = query.shape
    prefix = pkv.shape[1]
    every = prefix + rows
    pair = RATIO * HEAD_SIZE
    return pl.pallas_call(
        attention_kernel,
        grid=(KEY_VALUE_HEADS,),
        in_specs=[
            pl.BlockSpec(memory_space=pltpu.SMEM),
            pl.BlockSpec((1, rows), lambda i: (0, 0)),
            pl.BlockSpec((rows, pair), lambda i: (0, i)),
            pl.BlockSpec((rows, pair), lambda i: (0, i)),
            pl.BlockSpec((2, rows, HEAD_SIZE), lambda i: (0, 0, i)),
            pl.BlockSpec((2, prefix, HEAD_SIZE), lambda i: (0, 0, i)),
        ],
        out_specs=[
            pl.BlockSpec((rows, pair), lambda i: (0, i)),
            pl.BlockSpec((rows, pair), lambda i: (0, i)),
            pl.BlockSpec((2, rows, HEAD_SIZE), lambda i: (0, 0, i)),
            pl.BlockSpec((2, prefix, HEAD_SIZE), lambda i: (0, 0, i)),
        ],
        out_shape=[
            jax.ShapeDtypeStruct((rows, wide), jnp.bfloat16),
            jax.ShapeDtypeStruct((rows, wide), jnp.bfloat16),
            jax.ShapeDtypeStruct(kv.shape, jnp.bfloat16),
            jax.ShapeDtypeStruct(pkv.shape, jnp.float32),
        ],
        scratch_shapes=[
            pltpu.VMEM((rows, rows), jnp.float32),
            pltpu.VMEM((every, HEAD_SIZE), jnp.bfloat16),
            pltpu.VMEM((every, HEAD_SIZE), jnp.bfloat16),
            pltpu.VMEM((HEAD_SIZE, every), jnp.bfloat16),
            pltpu.VMEM((HEAD_SIZE, every), jnp.bfloat16),
            pltpu.VMEM((every, QB), jnp.float32),
            pltpu.VMEM((every, QB), jnp.float32),
            pltpu.VMEM((every, QB), jnp.bfloat16),
        ],
        compiler_params=pltpu.CompilerParams(vmem_limit_bytes=40 * 1024 * 1024),
        name="attention",
    )(lengths, ends, query, cotangent, kv, pkv)


def body(n_p, n_b, query, branch_kv, prefix_kv, cotangent, subtree_end, lengths):
    own = prefix_kv.shape
    gathered = gather_prefix(n_p, n_b, prefix_kv)
    pkv = jnp.transpose(gathered, (1, 0, 2))
    kv = jnp.transpose(branch_kv[0], (1, 0, 2))
    att, qg, kvg, pg = attention(lengths, subtree_end, query[0], cotangent[0], kv, pkv)
    term = jnp.transpose(pg, (1, 0, 2)).astype(jnp.bfloat16)
    size = own[0] * own[1] * own[2]
    mine = scatter_prefix(n_p, n_b, term.reshape(n_p * n_b, 16, size // 16))
    return att[None], qg[None], jnp.transpose(kvg, (1, 0, 2))[None], mine.reshape(own)


def solution(mesh):
    both = ("prompt", "branch")
    in_specs = (
        P(both, None, None),
        P(both, None, None, None),
        P(both, None, None),
        P(both, None, None),
        P(both, None),
        P(both),
    )
    out_specs = (
        P(both, None, None),
        P(both, None, None),
        P(both, None, None, None),
        P(both, None, None),
    )
    part = functools.partial(body, mesh.shape["prompt"], mesh.shape["branch"])
    return jax.shard_map(part, mesh=mesh, in_specs=in_specs, out_specs=out_specs, check_vma=False)
```

time: 374 us -> 74.4 us (0.20)
  matrix products: 133 us -> 0 us
  blocking collectives: 121 us -> 0 us
  local copies, waits for them, and re-layouts: 77.4 us -> 8.95 us
  Pallas kernels: 0 us -> 63.9 us
  loops' own time: 20.5 us -> 0 us
  other arithmetic: 17.1 us -> 0.07 us
    dot_general x56 -> x0, matrix products: 133 us -> none  [the longest x16 39 us: scores_for(): jnp.einsum('qrd,nd->rqn', queries, key_rows, preferred_element_type=jnp.f...]
    all_gather x1 -> x0, blocking collectives: 72.7 us -> none  [collect_prefix(): return lax.all_gather(prefix_kv, ('prompt', 'branch'), axis=0, tiled=True)]
    pallas_call x0 -> x3, Pallas kernels: none -> 63.9 us  [the longest x1 30.3 us: attention(): pl.pallas_call(attention_kernel, grid=(KEY_VALUE_HEADS,), in_specs=[pl.Bl...]
    unnamed x1 -> x0, blocking collectives: 48.3 us -> none
    dynamic_slice x48 -> x0, local copies, waits for them, and re-layouts: 43.8 us -> none  [the longest x16 24.8 us: body(): lax.map(backward_group, (group_index, context_outputs, totals))]
    another operation x2 -> x0, loops' own time: 20.5 us -> none  [the longest x1 10.5 us: body(): context_outputs, totals = lax.map(forward_group, group_index)]
    while x97 -> x0, local copies, waits for them, and re-layouts: 7.54 us -> none
    dynamic_update_slice x8 -> x0, other arithmetic: 7.14 us -> none  [body(): lax.map(backward_group, (group_index, context_outputs, totals))]
where the time goes in v1:
time: 74.4 us; the launch traced here: 74.3 us
  Pallas kernels  63.9 us (86%)
  local copies, waits for them, and re-layouts  8.95 us (12%)
  between operations  1.37 us (2%)
    pallas_call x1, Pallas kernels, attention(): pl.pallas_call(attention_kernel, grid=(KEY_VALUE_HEADS,), in_specs=[pl.Bl...  30.3 us
    pallas_call x1, Pallas kernels, gather_prefix(): pl.pallas_call(functools.partial(gather_kernel, n_p, n_b), out_shape=jax....  19.8 us
    pallas_call x1, Pallas kernels, scatter_prefix(): pl.pallas_call(functools.partial(scatter_kernel, n_p, n_b), out_shape=jax...  13.8 us
    unnamed x8, local copies, waits for them, and re-layouts  6.3 us

profile of v1, /device:TPU:0, one launch (start us, length us, event | category | flops | bytes accessed | tf_op | source)
XLA Modules:
  0.0 74.3 jit_solution(4697422325760575076)
XLA Ops:
  1.3 19.8 %gather_prefix.1 = bf16[128,2,1024]{2,1,0:T(2,128)(2,1)} custom-call(bf16[4,2,1024]{2,1,0:T(2,128)(2,1)} %src.1), custom_call_target="tpu_custom_call" | custom-call | tf_op jit(solution)/shard_map/gather_prefix/pallas_call | solution.py:81
  21.1 0.0 copy-start.2
  21.1 1.2 %copy.17 = bf16[128,2,1024]{2,0,1:T(8,128)(2,1)S(1)} copy(bf16[128,2,1024]{2,1,0:T(2,128)(2,1)} %gather_prefix.1) | data formatting | bytes 1048576 | tf_op jit(solution)/shard_map/gather_prefix/pallas_call | solution.py:81
  22.3 0.0 copy-start
  22.3 0.0 copy-start.1
  22.3 2.4 %copy.16 = bf16[1,512,2,1024]{3,1,2,0:T(8,128)(2,1)S(1)} copy(bf16[1,512,2,1024]{3,2,1,0:T(2,128)(2,1)} %param.7) | data formatting | bytes 4194304 | tf_op args[1]
  24.7 0.0 copy-done.2
  24.7 0.0 copy-done
  24.7 0.4 copy-done.1
  25.2 30.3 %attention.1 = (bf16[512,2048]{1,0:T(8,128)(2,1)}, bf16[512,2048]{1,0:T(8,128)(2,1)}, bf16[2,512,1024]{2,1,0:T(8,128)(2,1)S(1)}, f32[2,128,1024]{2,1,0:T(8,128)S(1)}) custom-call(s32[1]{0:T(128)S(6)} %copy.18.lens, s32[1,512]{1,0:T(1,128)S(1)} %copy-done.2, bf16[512,2048]{1,0:T(8,128)(2,1)S(1)} %bitcast.19, bf16[512,2048]{1,0:T(8,128)(2,1)S(1)} %bitcast.20, ...), custom_call_target="tpu_custom_call" | custom-call | tf_op jit(solution)/shard_map/attention/pallas_call | solution.py:261
  55.4 0.1 convert_bitcast_fusion
  55.5 0.5 copy.12
  56.0 0.3 reshape.14.term
  56.4 13.8 %scatter_prefix.1 = bf16[16,512]{1,0:T(8,128)(2,1)S(1)} custom-call(bf16[32,16,512]{2,1,0:T(8,128)(2,1)S(1)} %reshape.14.term), custom_call_target="tpu_custom_call" | custom-call | tf_op jit(solution)/shard_map/scatter_prefix/pallas_call | solution.py:156
  70.2 0.6 reshape.15
  70.8 3.5 %copy.13 = bf16[1,512,2,1024]{3,2,1,0:T(2,128)(2,1)} copy(bf16[1,512,2,1024]{3,1,2,0:T(8,128)(2,1)S(1)} %bitcast.21) | data formatting | bytes 4194304
Async XLA Ops:
  21.1 3.6 %copy-start.2 = (s32[1,512]{1,0:T(1,128)S(1)}, s32[1,512]{1,0:T(1,128)}, u32[]{:S(2)}) copy-start(s32[1,512]{1,0:T(1,128)} %ends.1) | copy-start | bytes 6148
  22.3 2.4 %copy-start = (bf16[1,512,2048]{2,1,0:T(8,128)(2,1)S(1)}, bf16[1,512,2048]{2,1,0:T(8,128)(2,1)}, u32[]{:S(2)}) copy-start(bf16[1,512,2048]{2,1,0:T(8,128)(2,1)} %param.6) | copy-start | bytes 6291460
  22.3 2.8 %copy-start.1 = (bf16[1,512,2048]{2,1,0:T(8,128)(2,1)S(1)}, bf16[1,512,2048]{2,1,0:T(8,128)(2,1)}, u32[]{:S(2)}) copy-start(bf16[1,512,2048]{2,1,0:T(8,128)(2,1)} %param.9) | copy-start | bytes 6291460

commit v2 on v0

v2 whole, which is shorter than its diff:
```python
import functools

import jax
import jax.numpy as jnp
from jax import lax
from jax.experimental import pallas as pl
from jax.experimental.pallas import tpu as pltpu
from jax.sharding import PartitionSpec as P

QUERY_HEADS = 16
KEY_VALUE_HEADS = 8
HEAD_SIZE = 128
RATIO = QUERY_HEADS // KEY_VALUE_HEADS

softcap = 50.0
query_scale = 144.0 ** (-0.5)
MESH = pl.DeviceIdType.MESH
QB = 256
KC = 128


def nt(a, b):
    return lax.dot_general(a, b, (((1,), (1,)), ((), ())), preferred_element_type=jnp.float32)


def nn(a, b):
    return jnp.dot(a, b, preferred_element_type=jnp.float32)


def attention_kernel(n_p, n_b, pair_count, lens, ends, q_ref, g_ref, kv_ref, own_ref, att, qg, kvg, pg,
                     mask, pick, lay, w_s, t_s, k_all, v_all, kt, vt, ds_s,
                     ahead, terms, carry, land, ag_send, ag_recv, rs_send, rs_recv):
    rows = q_ref.shape[0]
    prefix = pick.shape[1] // 2
    devices = n_p * n_b
    length = lens[0]
    step = pl.program_id(0)
    groups = KEY_VALUE_HEADS
    group = lax.rem(step, groups)
    blocks = rows // QB
    p, b = lax.axis_index("prompt"), lax.axis_index("branch")
    me = p * n_b + b

    def peer(k):
        return (lax.rem(p + k // n_b, n_p), lax.rem(b + lax.rem(k, n_b), n_b))

    def gather_copy(part, k):
        return pltpu.make_async_remote_copy(
            src_ref=own_ref.at[part], dst_ref=ahead.at[part, me],
            send_sem=ag_send.at[part, k], recv_sem=ag_recv.at[part, k],
            device_id=peer(k), device_id_type=MESH)

    def return_copy(part, k):
        to_p, to_b = peer(k)
        return pltpu.make_async_remote_copy(
            src_ref=terms.at[part, to_p * n_b + to_b], dst_ref=land.at[part, k],
            send_sem=rs_send.at[part, k], recv_sem=rs_recv.at[part, k],
            device_id=(to_p, to_b), device_id_type=MESH)

    def each(act):
        def turn(k, _):
            act(k)
            return 0
        lax.fori_loop(1, devices, turn, 0)

    @pl.when(step == 0)
    def _():
        barrier = pltpu.get_barrier_semaphore()
        each(lambda k: pl.semaphore_signal(barrier, inc=1, device_id=peer(k), device_id_type=MESH))
        for r in range(0, rows, KC):
            span = jnp.broadcast_to(ends[:, r:r + KC].astype(jnp.float32), (KC, KC))
            stop = jnp.transpose(span)[:, :1]
            t = lax.broadcasted_iota(jnp.int32, (KC, rows), 0) + r
            i = lax.broadcasted_iota(jnp.int32, (KC, rows), 1)
            seen = (t <= i) & (i.astype(jnp.float32) < stop)
            mask[r:r + KC, :] = jnp.where(seen, 1.0, 0.0)

    @pl.when(step == 2)
    def _():
        pl.semaphore_wait(pltpu.get_barrier_semaphore(), devices - 1)
        for part in range(pair_count):
            each(lambda k: gather_copy(part, k).start())
            ahead[part, me] = own_ref[part]

    @pl.when(step == 1)
    def _():
        per = prefix // devices
        half = 2 * per
        wide = pick.shape[2]
        for parity in range(2):
            row = lax.broadcasted_iota(jnp.int32, (2 * prefix, wide), 0)
            col = lax.broadcasted_iota(jnp.int32, (2 * prefix, wide), 1)
            kv = row // prefix
            at = row - kv * prefix
            want = (at // per) * (2 * half) + parity * half + kv * per + at % per
            pick[parity] = jnp.where(want == col, 1.0, 0.0).astype(jnp.bfloat16)
            row = lax.broadcasted_iota(jnp.int32, (wide, 2 * prefix), 0)
            col = lax.broadcasted_iota(jnp.int32, (wide, 2 * prefix), 1)
            kv = col // prefix
            at = col - kv * prefix
            want = (at // per) * (2 * half) + parity * half + kv * per + at % per
            lay[parity] = jnp.where(want == row, 1.0, 0.0).astype(jnp.bfloat16)

    units = []
    base = 0
    for h in range(RATIO):
        for j in range(blocks):
            units.append((h, j, base))
            base += (j + 1) * QB

    @pl.when(step < groups)
    def _():
        for h, j, base in units:
            cols = slice(h * HEAD_SIZE, (h + 1) * HEAD_SIZE)
            spot = slice(j * QB, (j + 1) * QB)
            q = q_ref[spot, cols]
            for c in range((j + 1) * QB // KC):
                at = slice(c * KC, (c + 1) * KC)
                t = jnp.tanh(nt(kv_ref[0, at], q) * (query_scale / softcap))
                w = jnp.exp(softcap * t) * mask[at, spot]
                w_s[group, base + c * KC:base + (c + 1) * KC] = w
                t_s[group, base + c * KC:base + (c + 1) * KC] = t

    @pl.when((step >= groups) & (lax.rem(step, 2) == 0))
    def _():
        each(lambda k: gather_copy(group // 2, k).wait_recv())

    @pl.when(step >= groups)
    def _():
        part = group // 2
        parity = lax.rem(group, 2)
        arrived = ahead[part].reshape(pick.shape[2], HEAD_SIZE)
        prompt_rows = nn(pick[parity], arrived).astype(jnp.bfloat16)
        k_all[:prefix] = prompt_rows[:prefix]
        k_all[prefix:] = kv_ref[0]
        v_all[:prefix] = prompt_rows[prefix:]
        v_all[prefix:] = kv_ref[1]
        kt[...] = jnp.transpose(k_all[...])
        vt[...] = jnp.transpose(v_all[...])

        dk = [None] * ((prefix + rows) // KC)
        dv = [None] * ((prefix + rows) // KC)
        for h, j, base in units:
            cols = slice(h * HEAD_SIZE, (h + 1) * HEAD_SIZE)
            spot = slice(j * QB, (j + 1) * QB)
            n = prefix + (j + 1) * QB
            chunks = n // KC
            live = lax.broadcasted_iota(jnp.int32, (QB, HEAD_SIZE), 0) + j * QB < length
            q = q_ref[spot, cols]
            g = jnp.where(live, g_ref[spot, cols], jnp.zeros((), jnp.bfloat16))
            total = jnp.zeros((1, QB), jnp.float32)
            first = {}
            for c in range(chunks):
                if c * KC < prefix:
                    t = jnp.tanh(nt(k_all[c * KC:(c + 1) * KC], q) * (query_scale / softcap))
                    w = jnp.exp(softcap * t)
                    first[c] = (w, t)
                else:
                    w = w_s[group, base + c * KC - prefix:base + (c + 1) * KC - prefix]
                total += jnp.sum(w, axis=0, keepdims=True)
            inverse = 1.0 / total

            def weights(c):
                if c in first:
                    return first[c]
                at = slice(base + c * KC - prefix, base + (c + 1) * KC - prefix)
                return w_s[group, at], t_s[group, at]

            probs = []
            for c in range(chunks):
                probs.append((weights(c)[0] * inverse).astype(jnp.bfloat16))
            probs = jnp.concatenate(probs, axis=0)
            context = nn(vt[:, :n], probs)
            delta = jnp.sum(jnp.transpose(g).astype(jnp.float32) * context, axis=0, keepdims=True)
            att[spot, cols] = jnp.where(
                live, jnp.transpose(context.astype(jnp.bfloat16)), jnp.zeros((), jnp.bfloat16))
            for c in range(chunks):
                at = slice(c * KC, (c + 1) * KC)
                w, t = weights(c)
                score = (w * inverse) * (nt(v_all[at], g) - delta) * (1.0 - t * t)
                ds_s[at] = score.astype(jnp.bfloat16)
            scores = ds_s[:n]
            dq = nn(kt[:, :n], scores) * query_scale
            qg[spot, cols] = jnp.transpose(dq.astype(jnp.bfloat16))
            for c in range(chunks):
                at = slice(c * KC, (c + 1) * KC)
                one = nn(scores[at], q)
                two = nn(probs[at], g)
                dk[c] = one if dk[c] is None else dk[c] + one
                dv[c] = two if dv[c] is None else dv[c] + two
        sums = []
        for c in range(len(dk)):
            if c * KC < prefix:
                sums.append((dk[c], dv[c]))
            else:
                at = slice(c * KC - prefix, (c + 1) * KC - prefix)
                kvg[0, at] = (dk[c] * query_scale).astype(jnp.bfloat16)
                kvg[1, at] = dv[c].astype(jnp.bfloat16)
        stack = jnp.concatenate([s[0] * query_scale for s in sums] + [s[1] for s in sums], axis=0)
        placed = nn(lay[parity], stack.astype(jnp.bfloat16))

        @pl.when(parity == 0)
        def _():
            carry[...] = placed

        @pl.when(parity == 1)
        def _():
            terms[part] = (carry[...] + placed).astype(jnp.bfloat16).reshape(terms.shape[1:])
            each(lambda k: return_copy(part, k).start())

    @pl.when(step == 2 * groups - 1)
    def _():
        for part in range(pair_count):
            each(lambda k: gather_copy(part, k).wait_send())
            total = terms[part, me].astype(jnp.float32)

            def turn(k, total):
                return_copy(part, k).wait()
                return total + land[part, k].astype(jnp.float32)

            total = lax.fori_loop(1, devices, turn, total)
            pg[part] = total.astype(jnp.bfloat16)


def attention(n_p, n_b, lengths, ends, query, cotangent, kv, own):
    rows, wide = query.shape
    devices = n_p * n_b
    pair_count, high, _ = own.shape
    prefix = devices * (high // 4)
    every = prefix + rows
    pair = RATIO * HEAD_SIZE
    groups = KEY_VALUE_HEADS
    blocks = rows // QB
    stored = RATIO * QB * blocks * (blocks + 1) // 2
    late = lambda i: (0, (i // groups) * (i % groups))
    late3 = lambda i: (0, 0, (i // groups) * (i % groups))
    bf16, f32 = jnp.bfloat16, jnp.float32
    return pl.pallas_call(
        functools.partial(attention_kernel, n_p, n_b, pair_count),
        grid=(2 * groups,),
        in_specs=[
            pl.BlockSpec(memory_space=pltpu.SMEM),
            pl.BlockSpec((1, rows), lambda i: (0, 0)),
            pl.BlockSpec((rows, pair), lambda i: (0, i % groups)),
            pl.BlockSpec((rows, pair), late),
            pl.BlockSpec((2, rows, HEAD_SIZE), lambda i: (0, 0, i % groups)),
            pl.BlockSpec(memory_space=pltpu.VMEM),
        ],
        out_specs=[
            pl.BlockSpec((rows, pair), late),
            pl.BlockSpec((rows, pair), late),
            pl.BlockSpec((2, rows, HEAD_SIZE), late3),
            pl.BlockSpec((pair_count, high, HEAD_SIZE), lambda i: (0, 0, 0)),
        ],
        out_shape=[
            jax.ShapeDtypeStruct((rows, wide), bf16),
            jax.ShapeDtypeStruct((rows, wide), bf16),
            jax.ShapeDtypeStruct(kv.shape, bf16),
            jax.ShapeDtypeStruct(own.shape, bf16),
        ],
        scratch_shapes=[
            pltpu.VMEM((rows, rows), f32),
            pltpu.VMEM((2, 2 * prefix, devices * high), bf16),
            pltpu.VMEM((2, devices * high, 2 * prefix), bf16),
            pltpu.VMEM((groups, stored, QB), f32),
            pltpu.VMEM((groups, stored, QB), f32),
            pltpu.VMEM((every, HEAD_SIZE), bf16),
            pltpu.VMEM((every, HEAD_SIZE), bf16),
            pltpu.VMEM((HEAD_SIZE, every), bf16),
            pltpu.VMEM((HEAD_SIZE, every), bf16),
            pltpu.VMEM((every, QB), bf16),
            pltpu.VMEM((pair_count, devices, high, HEAD_SIZE), bf16),
            pltpu.VMEM((pair_count, devices, high, HEAD_SIZE), bf16),
            pltpu.VMEM((devices * high, HEAD_SIZE), f32),
            pltpu.VMEM((pair_count, devices, high, HEAD_SIZE), bf16),
            pltpu.SemaphoreType.DMA((pair_count, devices)),
            pltpu.SemaphoreType.DMA((pair_count, devices)),
            pltpu.SemaphoreType.DMA((pair_count, devices)),
            pltpu.SemaphoreType.DMA((pair_count, devices)),
        ],
        compiler_params=pltpu.CompilerParams(
            collective_id=0, has_side_effects=True, vmem_limit_bytes=58 * 1024 * 1024),
        name="attention",
    )(lengths, ends, query, cotangent, kv, own)


def body(n_p, n_b, query, branch_kv, prefix_kv, cotangent, subtree_end, lengths):
    per = prefix_kv.shape[0]
    pairs = KEY_VALUE_HEADS // 2
    own = jnp.transpose(prefix_kv.reshape(per, 2, pairs, 2, HEAD_SIZE), (2, 3, 1, 0, 4))
    own = own.reshape(pairs, 4 * per, HEAD_SIZE)
    kv = jnp.transpose(branch_kv[0], (1, 0, 2))
    att, qg, kvg, pg = attention(n_p, n_b, lengths, subtree_end, query[0], cotangent[0], kv, own)
    mine = jnp.transpose(pg.reshape(pairs, 2, 2, per, HEAD_SIZE), (3, 2, 0, 1, 4))
    return att[None], qg[None], jnp.transpose(kvg, (1, 0, 2))[None], mine.reshape(prefix_kv.shape)


def solution(mesh):
    both = ("prompt", "branch")
    in_specs = (
        P(both, None, None),
        P(both, None, None, None),
        P(both, None, None),
        P(both, None, None),
        P(both, None),
        P(both),
    )
    out_specs = (
        P(both, None, None),
        P(both, None, None),
        P(both, None, None, None),
        P(both, None, None),
    )
    part = functools.partial(body, mesh.shape["prompt"], mesh.shape["branch"])
    return jax.shard_map(part, mesh=mesh, in_specs=in_specs, out_specs=out_specs, check_vma=False)
```

time: 374 us -> 71.5 us (0.19)
  matrix products: 133 us -> 0 us
  blocking collectives: 121 us -> 0 us
  local copies, waits for them, and re-layouts: 77.4 us -> 15.1 us
  Pallas kernels: 0 us -> 54.7 us
  loops' own time: 20.5 us -> 0 us
  other arithmetic: 17.1 us -> 0 us
    dot_general x56 -> x0, matrix products: 133 us -> none  [the longest x16 39 us: scores_for(): jnp.einsum('qrd,nd->rqn', queries, key_rows, preferred_element_type=jnp.f...]
    all_gather x1 -> x0, blocking collectives: 72.7 us -> none  [collect_prefix(): return lax.all_gather(prefix_kv, ('prompt', 'branch'), axis=0, tiled=True)]
    pallas_call x0 -> x1, Pallas kernels: none -> 54.7 us  [attention(): pl.pallas_call(functools.partial(attention_kernel, n_p, n_b, pair_count),...]
    unnamed x1 -> x0, blocking collectives: 48.3 us -> none
    dynamic_slice x48 -> x0, local copies, waits for them, and re-layouts: 43.8 us -> none  [the longest x16 24.8 us: body(): lax.map(backward_group, (group_index, context_outputs, totals))]
    another operation x2 -> x0, loops' own time: 20.5 us -> none  [the longest x1 10.5 us: body(): context_outputs, totals = lax.map(forward_group, group_index)]
    while x97 -> x0, local copies, waits for them, and re-layouts: 7.54 us -> none
    dynamic_update_slice x8 -> x0, other arithmetic: 7.14 us -> none  [body(): lax.map(backward_group, (group_index, context_outputs, totals))]
where the time goes in v2:
time: 71.5 us; the launch traced here: 71.1 us
  Pallas kernels  54.7 us (77%)
  local copies, waits for them, and re-layouts  15.1 us (21%)
  between operations  1.29 us (2%)
    pallas_call x1, Pallas kernels, attention(): pl.pallas_call(functools.partial(attention_kernel, n_p, n_b, pair_count),...  54.7 us
    unnamed x8, local copies, waits for them, and re-layouts  12.4 us

profile of v2, /device:TPU:0, one launch (start us, length us, event | category | flops | bytes accessed | tf_op | source)
XLA Modules:
  0.0 71.1 jit_solution(15182972374780268159)
XLA Ops:
  1.3 0.7 %reshape.20 = bf16[4,2,4,2,128]{4,3,2,1,0:T(2,128)(2,1)S(1)} reshape(bf16[4,2,1024]{2,1,0:T(2,128)(2,1)} %param.8) | data formatting | bytes 32768 | tf_op jit(solution)/shard_map/reshape | solution.py:290
  2.0 0.6 copy.11
  2.6 3.5 %copy.15 = bf16[1,512,2,1024]{3,1,2,0:T(8,128)(2,1)} copy(bf16[1,512,2,1024]{3,2,1,0:T(2,128)(2,1)} %param.7) | data formatting | bytes 4194304 | tf_op args[1]
  6.2 54.7 %attention.1 = (bf16[512,2048]{1,0:T(8,128)(2,1)}, bf16[512,2048]{1,0:T(8,128)(2,1)}, bf16[2,512,1024]{2,1,0:T(8,128)(2,1)}, bf16[4,16,128]{2,1,0:T(8,128)(2,1)}) custom-call(s32[1]{0:T(128)S(6)} %copy.18.lens, s32[1,512]{1,0:T(1,128)} %ends.1, bf16[512,2048]{1,0:T(8,128)(2,1)} %bitcast.19, bf16[512,2048]{1,0:T(8,128)(2,1)} %bitcast.20, ...), custom_call_target="tpu_custom_call" | custom-call | tf_op jit(solution)/shard_map/attention/pallas_call | solution.py:238
  60.8 0.7 %copy.12 = bf16[4,2,4,2,128]{4,3,2,1,0:T(2,128)(2,1)S(1)} copy(bf16[4,2,4,2,128]{4,0,1,3,2:T(4,128)(2,1)} %bitcast.25) | data formatting | bytes 32768 | tf_op jit(solution)/shard_map/transpose | solution.py:294
  61.6 0.6 reshape.23
  62.2 0.0 copy-start.1
  62.2 5.2 %copy.13 = bf16[1,512,2,1024]{3,2,1,0:T(2,128)(2,1)} copy(bf16[1,512,2,1024]{3,1,2,0:T(8,128)(2,1)} %bitcast.23) | data formatting | bytes 4194304
  67.4 0.0 copy-done.1
  67.4 0.0 copy-start
  67.4 1.3 %copy.19 = bf16[1,512,2048]{2,1,0:T(8,128)(2,1)} copy(bf16[1,512,2048]{2,1,0:T(8,128)(2,1)S(1)} %bitcast.22) | data formatting | bytes 4194304
  68.7 1.0 %copy-done = bf16[512,2048]{1,0:T(8,128)(2,1)S(1)} copy-done((bf16[512,2048]{1,0:T(8,128)(2,1)S(1)}, bf16[512,2048]{1,0:T(8,128)(2,1)}, u32[]{:S(2)}) %copy-start) | copy-done | bytes 2097176
  69.8 1.3 %copy.20 = bf16[1,512,2048]{2,1,0:T(8,128)(2,1)} copy(bf16[1,512,2048]{2,1,0:T(8,128)(2,1)S(1)} %bitcast.21) | data formatting | bytes 4194304
Async XLA Ops:
  62.2 5.2 %copy-start.1 = (bf16[512,2048]{1,0:T(8,128)(2,1)S(1)}, bf16[512,2048]{1,0:T(8,128)(2,1)}, u32[]{:S(2)}) copy-start(bf16[512,2048]{1,0:T(8,128)(2,1)} %get-tuple-element.8) | copy-start | bytes 6291460
  67.4 2.3 %copy-start = (bf16[512,2048]{1,0:T(8,128)(2,1)S(1)}, bf16[512,2048]{1,0:T(8,128)(2,1)}, u32[]{:S(2)}) copy-start(bf16[512,2048]{1,0:T(8,128)(2,1)} %get-tuple-element.9) | copy-start | bytes 6291460

commit v3 on v2

v3 whole, which is shorter than its diff:
```python
import functools

import jax
import jax.numpy as jnp
from jax import lax
from jax.experimental import pallas as pl
from jax.experimental.pallas import tpu as pltpu
from jax.sharding import PartitionSpec as P

QUERY_HEADS = 16
KEY_VALUE_HEADS = 8
HEAD_SIZE = 128
RATIO = QUERY_HEADS // KEY_VALUE_HEADS

softcap = 50.0
query_scale = 144.0 ** (-0.5)
MESH = pl.DeviceIdType.MESH
QB = 256
KC = 128


def nt(a, b):
    return lax.dot_general(a, b, (((1,), (1,)), ((), ())), preferred_element_type=jnp.float32)


def nn(a, b):
    return jnp.dot(a, b, preferred_element_type=jnp.float32)


def attention_kernel(n_p, n_b, pair_count, lens, ends, q_ref, g_ref, kv_ref, own_ref, att, qg, kvg, pg,
                     mask, pick, lay, w_s, t_s, d_s, k_s, v_s, kt_s, vt_s,
                     ahead, terms, carry, land, ag_send, ag_recv, rs_send, rs_recv):
    rows = q_ref.shape[0]
    devices = n_p * n_b
    high = own_ref.shape[1]
    prefix = devices * high // 4
    some = pick.shape[1] // 2
    wide = pick.shape[2]
    length = lens[0]
    step = pl.program_id(0)
    groups = KEY_VALUE_HEADS
    group = lax.rem(step, groups)
    blocks = rows // QB
    p, b = lax.axis_index("prompt"), lax.axis_index("branch")
    me = p * n_b + b

    def peer(k):
        return (lax.rem(p + k // n_b, n_p), lax.rem(b + k % n_b, n_b))

    def gather_copy(part, k):
        return pltpu.make_async_remote_copy(
            src_ref=own_ref.at[part], dst_ref=ahead.at[part, me],
            send_sem=ag_send.at[part], recv_sem=ag_recv.at[part],
            device_id=peer(k), device_id_type=MESH)

    def return_copy(part, k):
        to_p, to_b = peer(k)
        return pltpu.make_async_remote_copy(
            src_ref=terms.at[part, to_p * n_b + to_b], dst_ref=land.at[part, k],
            send_sem=rs_send.at[part], recv_sem=rs_recv.at[part],
            device_id=(to_p, to_b), device_id_type=MESH)

    def each(act):
        for k in range(1, devices):
            act(k)

    def settle(buffer, sem):
        span = buffer.at[pl.ds(0, devices - 1)]
        pltpu.make_async_copy(span, span, sem).wait()

    @pl.when(step == 0)
    def _():
        barrier = pltpu.get_barrier_semaphore()
        each(lambda k: pl.semaphore_signal(barrier, inc=1, device_id=peer(k), device_id_type=MESH))
        for r in range(0, rows, KC):
            span = jnp.broadcast_to(ends[:, r:r + KC].astype(jnp.float32), (KC, KC))
            stop = jnp.transpose(span)[:, :1]
            t = lax.broadcasted_iota(jnp.int32, (KC, rows), 0) + r
            i = lax.broadcasted_iota(jnp.int32, (KC, rows), 1)
            seen = (t <= i) & (i.astype(jnp.float32) < stop)
            mask[r:r + KC, :] = jnp.where(seen, 1.0, 0.0)

    def gather_start(part):
        each(lambda k: gather_copy(part, k).start())
        ahead[part, me] = own_ref[part]

    @pl.when(step == 4)
    def _():
        pl.semaphore_wait(pltpu.get_barrier_semaphore(), devices - 1)

    for part in range(pair_count):
        @pl.when(step == 4 + 2 * part)
        def _():
            gather_start(part)

    @pl.when(step == 1)
    def _():
        per = high // 4

        def place(shape, dim):
            line = lax.broadcasted_iota(jnp.int32, shape, dim)
            kv = line // some
            at = line - kv * some
            return (at // per) * (4 * per) + kv * per + at % per

        down = place((2 * some, 1), 0)
        over = place((1, 2 * some), 1)
        col = lax.broadcasted_iota(jnp.int32, (2 * some, wide), 1)
        row = lax.broadcasted_iota(jnp.int32, (wide, 2 * some), 0)
        for parity in range(2):
            shift = parity * 2 * per
            pick[parity] = jnp.where(down + shift == col, 1.0, 0.0).astype(jnp.bfloat16)
            lay[parity] = jnp.where(over + shift == row, 1.0, 0.0).astype(jnp.bfloat16)

    units = []
    base = 0
    for h in range(RATIO):
        for j in range(blocks):
            units.append((h, j, base))
            base += (j + 1) * QB

    def live_rows(j):
        return lax.broadcasted_iota(jnp.int32, (QB, HEAD_SIZE), 0) + j * QB < length

    def masked(j, spot, cols):
        return jnp.where(live_rows(j), g_ref[spot, cols], jnp.zeros((), jnp.bfloat16))

    @pl.when(step < groups)
    def _():
        keys = kv_ref[:, 0, :]
        values = kv_ref[:, 1, :]
        k_s[group] = keys
        v_s[group] = values
        kt_s[group] = jnp.transpose(keys)
        vt_s[group] = jnp.transpose(values)
        for h, j, base in units:
            cols = slice(h * HEAD_SIZE, (h + 1) * HEAD_SIZE)
            spot = slice(j * QB, (j + 1) * QB)
            q = q_ref[spot, cols]
            g = masked(j, spot, cols)
            for c in range((j + 1) * QB // KC):
                at = slice(c * KC, (c + 1) * KC)
                to = slice(base + c * KC, base + (c + 1) * KC)
                t = jnp.tanh(nt(keys[at], q) * (query_scale / softcap))
                w_s[group, to] = jnp.exp(softcap * t) * mask[at, spot]
                t_s[group, to] = t
                d_s[group, to] = nt(values[at], g)

    @pl.when((step >= groups) & (lax.rem(step, 2) == 0))
    def _():
        settle(ahead.at[group // 2], ag_recv.at[group // 2])

    @pl.when(step >= groups)
    def _():
        part = group // 2
        parity = lax.rem(group, 2)
        key_parts, value_parts = [], []
        for one in range(prefix // some):
            arrived = ahead[part, one * (wide // high):(one + 1) * (wide // high)].reshape(wide, HEAD_SIZE)
            lines = nn(pick[parity], arrived).astype(jnp.bfloat16)
            key_parts.append(lines[:some])
            value_parts.append(lines[some:])
        prompt_keys = jnp.concatenate(key_parts, axis=0)
        prompt_values = jnp.concatenate(value_parts, axis=0)
        prompt_kt = jnp.transpose(prompt_keys)
        prompt_vt = jnp.transpose(prompt_values)

        dk = [None] * ((prefix + rows) // KC)
        dv = [None] * ((prefix + rows) // KC)
        for h, j, base in units:
            cols = slice(h * HEAD_SIZE, (h + 1) * HEAD_SIZE)
            spot = slice(j * QB, (j + 1) * QB)
            tree = (j + 1) * QB
            chunks = (prefix + tree) // KC
            q = q_ref[spot, cols]
            g = masked(j, spot, cols)
            total = jnp.zeros((1, QB), jnp.float32)
            first = {}
            for c in range(chunks):
                if c * KC < prefix:
                    at = slice(c * KC, (c + 1) * KC)
                    t = jnp.tanh(nt(prompt_keys[at], q) * (query_scale / softcap))
                    w = jnp.exp(softcap * t)
                    first[c] = (w, t, nt(prompt_values[at], g))
                else:
                    w = w_s[group, base + c * KC - prefix:base + (c + 1) * KC - prefix]
                total += jnp.sum(w, axis=0, keepdims=True)
            inverse = 1.0 / total

            def weights(c):
                if c in first:
                    return first[c]
                at = slice(base + c * KC - prefix, base + (c + 1) * KC - prefix)
                return w_s[group, at], t_s[group, at], d_s[group, at]

            near = prefix // KC
            probs = [(weights(c)[0] * inverse).astype(jnp.bfloat16) for c in range(chunks)]
            context = nn(prompt_vt, jnp.concatenate(probs[:near], axis=0))
            context += nn(vt_s[group, :, :tree], jnp.concatenate(probs[near:], axis=0))
            delta = jnp.sum(jnp.transpose(g).astype(jnp.float32) * context, axis=0, keepdims=True)
            att[spot, cols] = jnp.where(
                live_rows(j), jnp.transpose(context.astype(jnp.bfloat16)), jnp.zeros((), jnp.bfloat16))
            scores = []
            for c in range(chunks):
                w, t, d = weights(c)
                scores.append(((w * inverse) * (d - delta) * (1.0 - t * t)).astype(jnp.bfloat16))
            dq = nn(prompt_kt, jnp.concatenate(scores[:near], axis=0))
            dq += nn(kt_s[group, :, :tree], jnp.concatenate(scores[near:], axis=0))
            qg[spot, cols] = jnp.transpose((dq * query_scale).astype(jnp.bfloat16))
            for c in range(chunks):
                one = nn(scores[c], q)
                two = nn(probs[c], g)
                dk[c] = one if dk[c] is None else dk[c] + one
                dv[c] = two if dv[c] is None else dv[c] + two
        sums = []
        for c in range(len(dk)):
            if c * KC < prefix:
                sums.append((dk[c], dv[c]))
            else:
                at = slice(c * KC - prefix, (c + 1) * KC - prefix)
                kvg[0, at] = (dk[c] * query_scale).astype(jnp.bfloat16)
                kvg[1, at] = dv[c].astype(jnp.bfloat16)
        all_k = jnp.concatenate([one[0] for one in sums], axis=0) * query_scale
        all_v = jnp.concatenate([one[1] for one in sums], axis=0)
        placed = []
        for one in range(prefix // some):
            at = slice(one * some, (one + 1) * some)
            stack = jnp.concatenate([all_k[at], all_v[at]], axis=0)
            placed.append(nn(lay[parity], stack.astype(jnp.bfloat16)))
        placed = jnp.concatenate(placed, axis=0)

        @pl.when(parity == 0)
        def _():
            carry[...] = placed

        @pl.when(parity == 1)
        def _():
            terms[part] = (carry[...] + placed).astype(jnp.bfloat16).reshape(terms.shape[1:])
            each(lambda k: return_copy(part, k).start())

    @pl.when(step == 2 * groups - 1)
    def _():
        for part in range(pair_count):
            settle(ahead.at[part], ag_send.at[part])
            settle(terms.at[part], rs_send.at[part])
            settle(land.at[part], rs_recv.at[part])
            total = terms[part, me].astype(jnp.float32)
            for k in range(1, devices):
                total += land[part, k].astype(jnp.float32)
            pg[part] = total.astype(jnp.bfloat16)


def attention(n_p, n_b, lengths, ends, query, cotangent, kv, own):
    rows, wide = query.shape
    devices = n_p * n_b
    pair_count, high, _ = own.shape
    prefix = devices * (high // 4)
    pair = RATIO * HEAD_SIZE
    groups = KEY_VALUE_HEADS
    blocks = rows // QB
    stored = RATIO * QB * blocks * (blocks + 1) // 2
    late = lambda i: (0, (i // groups) * (i % groups))
    late3 = lambda i: (0, 0, (i // groups) * (i % groups))
    early3 = lambda i: (0, 0, (1 - i // groups) * (i % groups) + (i // groups) * (groups - 1))
    some = prefix // max(devices // 32, 1)
    wide_pair = 4 * some
    bf16, f32 = jnp.bfloat16, jnp.float32
    return pl.pallas_call(
        functools.partial(attention_kernel, n_p, n_b, pair_count),
        grid=(2 * groups,),
        in_specs=[
            pl.BlockSpec(memory_space=pltpu.SMEM),
            pl.BlockSpec((1, rows), lambda i: (0, 0)),
            pl.BlockSpec((rows, pair), lambda i: (0, i % groups)),
            pl.BlockSpec((rows, pair), lambda i: (0, i % groups)),
            pl.BlockSpec((rows, 2, HEAD_SIZE), early3),
            pl.BlockSpec(memory_space=pltpu.VMEM),
        ],
        out_specs=[
            pl.BlockSpec((rows, pair), late),
            pl.BlockSpec((rows, pair), late),
            pl.BlockSpec((2, rows, HEAD_SIZE), late3),
            pl.BlockSpec((pair_count, high, HEAD_SIZE), lambda i: (0, 0, 0)),
        ],
        out_shape=[
            jax.ShapeDtypeStruct((rows, wide), bf16),
            jax.ShapeDtypeStruct((rows, wide), bf16),
            jax.ShapeDtypeStruct((2, rows, kv.shape[2]), bf16),
            jax.ShapeDtypeStruct(own.shape, bf16),
        ],
        scratch_shapes=[
            pltpu.VMEM((rows, rows), f32),
            pltpu.VMEM((2, 2 * some, wide_pair), bf16),
            pltpu.VMEM((2, wide_pair, 2 * some), bf16),
            pltpu.VMEM((groups, stored, QB), f32),
            pltpu.VMEM((groups, stored, QB), f32),
            pltpu.VMEM((groups, stored, QB), f32),
            pltpu.VMEM((groups, rows, HEAD_SIZE), bf16),
            pltpu.VMEM((groups, rows, HEAD_SIZE), bf16),
            pltpu.VMEM((groups, HEAD_SIZE, rows), bf16),
            pltpu.VMEM((groups, HEAD_SIZE, rows), bf16),
            pltpu.VMEM((pair_count, devices, high, HEAD_SIZE), bf16),
            pltpu.VMEM((pair_count, devices, high, HEAD_SIZE), bf16),
            pltpu.VMEM((devices * high, HEAD_SIZE), f32),
            pltpu.VMEM((pair_count, devices, high, HEAD_SIZE), bf16),
            pltpu.SemaphoreType.DMA((pair_count,)),
            pltpu.SemaphoreType.DMA((pair_count,)),
            pltpu.SemaphoreType.DMA((pair_count,)),
            pltpu.SemaphoreType.DMA((pair_count,)),
        ],
        compiler_params=pltpu.CompilerParams(
            collective_id=0, has_side_effects=True, vmem_limit_bytes=58 * 1024 * 1024),
        name="attention",
    )(lengths, ends, query, cotangent, kv, own)


def body(n_p, n_b, query, branch_kv, prefix_kv, cotangent, subtree_end, lengths):
    per = prefix_kv.shape[0]
    pairs = KEY_VALUE_HEADS // 2
    own = jnp.transpose(prefix_kv.reshape(per, 2, pairs, 2, HEAD_SIZE), (2, 3, 1, 0, 4))
    own = own.reshape(pairs, 4 * per, HEAD_SIZE)
    kv = branch_kv[0]
    att, qg, kvg, pg = attention(n_p, n_b, lengths, subtree_end, query[0], cotangent[0], kv, own)
    mine = jnp.transpose(pg.reshape(pairs, 2, 2, per, HEAD_SIZE), (3, 2, 0, 1, 4))
    return att[None], qg[None], jnp.transpose(kvg, (1, 0, 2))[None], mine.reshape(prefix_kv.shape)


def solution(mesh):
    both = ("prompt", "branch")
    in_specs = (
        P(both, None, None),
        P(both, None, None, None),
        P(both, None, None),
        P(both, None, None),
        P(both, None),
        P(both),
    )
    out_specs = (
        P(both, None, None),
        P(both, None, None),
        P(both, None, None, None),
        P(both, None, None),
    )
    part = functools.partial(body, mesh.shape["prompt"], mesh.shape["branch"])
    return jax.shard_map(part, mesh=mesh, in_specs=in_specs, out_specs=out_specs, check_vma=False)
```

time: 71.5 us -> 61.5 us (0.86)
  Pallas kernels: 54.7 us -> 48.3 us
  local copies, waits for them, and re-layouts: 15.1 us -> 11.6 us
    pallas_call x1, Pallas kernels: 54.7 us -> 48.3 us  [attention(): pl.pallas_call(functools.partial(attention_kernel, n_p, n_b, pair_count),...]
    unnamed x8 -> x7, local copies, waits for them, and re-layouts: 12.4 us -> 8.88 us
where the time goes in v3:
time: 61.5 us; the launch traced here: 61.2 us
  Pallas kernels  48.3 us (79%)
  local copies, waits for them, and re-layouts  11.6 us (19%)
  between operations  1.29 us (2%)
    pallas_call x1, Pallas kernels, attention(): pl.pallas_call(functools.partial(attention_kernel, n_p, n_b, pair_count),...  48.3 us
    unnamed x7, local copies, waits for them, and re-layouts  8.88 us
    reshape x2, local copies, waits for them, and re-layouts, body(): prefix_kv.reshape(per, 2, pairs, 2, HEAD_SIZE)  1.35 us

profile of v3, /device:TPU:0, one launch (start us, length us, event | category | flops | bytes accessed | tf_op | source)
XLA Modules:
  0.0 61.2 jit_solution(15091784178375542253)
XLA Ops:
  1.3 0.7 %reshape.20 = bf16[4,2,4,2,128]{4,3,2,1,0:T(2,128)(2,1)S(1)} reshape(bf16[4,2,1024]{2,1,0:T(2,128)(2,1)} %param.8) | data formatting | bytes 32768 | tf_op jit(solution)/shard_map/reshape | solution.py:320
  2.0 0.6 %copy.10 = bf16[4,2,4,2,128]{4,0,1,3,2:T(4,128)(2,1)} copy(bf16[4,2,4,2,128]{4,3,2,1,0:T(2,128)(2,1)S(1)} %reshape.20) | data formatting | bytes 32768 | tf_op jit(solution)/shard_map/reshape | solution.py:320
  2.6 48.3 %attention.1 = (bf16[512,2048]{1,0:T(8,128)(2,1)}, bf16[512,2048]{1,0:T(8,128)(2,1)}, bf16[2,512,1024]{2,1,0:T(8,128)(2,1)}, bf16[4,16,128]{2,1,0:T(8,128)(2,1)}) custom-call(s32[1]{0:T(128)S(6)} %copy.15.lens, s32[1,512]{1,0:T(1,128)} %ends.1, bf16[512,2048]{1,0:T(8,128)(2,1)} %bitcast.14, bf16[512,2048]{1,0:T(8,128)(2,1)} %bitcast.15, ...), custom_call_target="tpu_custom_call" | custom-call | tf_op jit(solution)/shard_map/attention/pallas_call | solution.py:268
  50.9 0.7 %copy.11 = bf16[4,2,4,2,128]{4,3,2,1,0:T(2,128)(2,1)S(1)} copy(bf16[4,2,4,2,128]{4,0,1,3,2:T(4,128)(2,1)} %bitcast.21) | data formatting | bytes 32768 | tf_op jit(solution)/shard_map/transpose | solution.py:324
  51.7 0.6 %reshape.23 = bf16[4,2,1024]{2,1,0:T(2,128)(2,1)} reshape(bf16[4,2,4,2,128]{4,3,2,1,0:T(2,128)(2,1)S(1)} %copy.11) | data formatting | bytes 32768 | tf_op jit(solution)/shard_map/reshape | solution.py:325
  52.3 0.0 copy-start.1
  52.3 5.2 %copy.12 = bf16[1,512,2,1024]{3,2,1,0:T(2,128)(2,1)} copy(bf16[1,512,2,1024]{3,1,2,0:T(8,128)(2,1)} %bitcast.19) | data formatting | bytes 4194304
  57.5 0.0 copy-done.1
  57.5 0.0 copy-start
  57.5 1.3 %copy.16 = bf16[1,512,2048]{2,1,0:T(8,128)(2,1)} copy(bf16[1,512,2048]{2,1,0:T(8,128)(2,1)S(1)} %bitcast.18) | data formatting | bytes 4194304
  58.8 1.0 %copy-done = bf16[512,2048]{1,0:T(8,128)(2,1)S(1)} copy-done((bf16[512,2048]{1,0:T(8,128)(2,1)S(1)}, bf16[512,2048]{1,0:T(8,128)(2,1)}, u32[]{:S(2)}) %copy-start) | copy-done | bytes 2097176
  59.9 1.3 %copy.17 = bf16[1,512,2048]{2,1,0:T(8,128)(2,1)} copy(bf16[1,512,2048]{2,1,0:T(8,128)(2,1)S(1)} %bitcast.17) | data formatting | bytes 4194304
Async XLA Ops:
  52.3 5.2 %copy-start.1 = (bf16[512,2048]{1,0:T(8,128)(2,1)S(1)}, bf16[512,2048]{1,0:T(8,128)(2,1)}, u32[]{:S(2)}) copy-start(bf16[512,2048]{1,0:T(8,128)(2,1)} %get-tuple-element.8) | copy-start | bytes 6291460
  57.5 2.3 %copy-start = (bf16[512,2048]{1,0:T(8,128)(2,1)S(1)}, bf16[512,2048]{1,0:T(8,128)(2,1)}, u32[]{:S(2)}) copy-start(bf16[512,2048]{1,0:T(8,128)(2,1)} %get-tuple-element.9) | copy-start | bytes 6291460

commit v4 on v3

--- a/solution.py
+++ b/solution.py
@@ -49,7 +49,7 @@
 
     def gather_copy(part, k):
         return pltpu.make_async_remote_copy(
-            src_ref=own_ref.at[part], dst_ref=ahead.at[part, me],
+            src_ref=own_ref.at[pl.ds(2 * part, 2)], dst_ref=ahead.at[part, me],
             send_sem=ag_send.at[part], recv_sem=ag_recv.at[part],
             device_id=peer(k), device_id_type=MESH)
 
@@ -82,14 +82,14 @@
 
     def gather_start(part):
         each(lambda k: gather_copy(part, k).start())
-        ahead[part, me] = own_ref[part]
+        ahead[part, me] = own_ref[2 * part:2 * part + 2]
 
     @pl.when(step == 4)
     def _():
         pl.semaphore_wait(pltpu.get_barrier_semaphore(), devices - 1)
 
-    for part in range(pair_count):
-        @pl.when(step == 4 + 2 * part)
+    for part in range(pair_count // 2):
+        @pl.when(step == 4 + 4 * part)
         def _():
             gather_start(part)
 
@@ -146,9 +146,9 @@
                 t_s[group, to] = t
                 d_s[group, to] = nt(values[at], g)
 
-    @pl.when((step >= groups) & (lax.rem(step, 2) == 0))
-    def _():
-        settle(ahead.at[group // 2], ag_recv.at[group // 2])
+    @pl.when((step >= groups) & (lax.rem(step, 4) == 0))
+    def _():
+        settle(ahead.at[group // 4], ag_recv.at[group // 4])
 
     @pl.when(step >= groups)
     def _():
@@ -156,7 +156,7 @@
         parity = lax.rem(group, 2)
         key_parts, value_parts = [], []
         for one in range(prefix // some):
-            arrived = ahead[part, one * (wide // high):(one + 1) * (wide // high)].reshape(wide, HEAD_SIZE)
+            arrived = ahead[part // 2, one * (wide // high):(one + 1) * (wide // high), lax.rem(part, 2)].reshape(wide, HEAD_SIZE)
             lines = nn(pick[parity], arrived).astype(jnp.bfloat16)
             key_parts.append(lines[:some])
             value_parts.append(lines[some:])
@@ -241,7 +241,8 @@
     @pl.when(step == 2 * groups - 1)
     def _():
         for part in range(pair_count):
-            settle(ahead.at[part], ag_send.at[part])
+            if part % 2 == 0:
+                settle(ahead.at[part // 2], ag_send.at[part // 2])
             settle(terms.at[part], rs_send.at[part])
             settle(land.at[part], rs_recv.at[part])
             total = terms[part, me].astype(jnp.float32)
@@ -299,7 +300,7 @@
             pltpu.VMEM((groups, rows, HEAD_SIZE), bf16),
             pltpu.VMEM((groups, HEAD_SIZE, rows), bf16),
             pltpu.VMEM((groups, HEAD_SIZE, rows), bf16),
-            pltpu.VMEM((pair_count, devices, high, HEAD_SIZE), bf16),
+            pltpu.VMEM((pair_count // 2, devices, 2, high, HEAD_SIZE), bf16),
             pltpu.VMEM((pair_count, devices, high, HEAD_SIZE), bf16),
             pltpu.VMEM((devices * high, HEAD_SIZE), f32),
             pltpu.VMEM((pair_count, devices, high, HEAD_SIZE), bf16),

time: 61.5 us -> 62.5 us (1.016)
  Pallas kernels: 48.3 us -> 49.3 us
    pallas_call x1, Pallas kernels: 48.3 us -> 49.3 us  [attention(): pl.pallas_call(functools.partial(attention_kernel, n_p, n_b, pair_count),...]
where the time goes in v4:
time: 62.5 us; the launch traced here: 62.2 us
  Pallas kernels  49.3 us (79%)
  local copies, waits for them, and re-layouts  11.6 us (19%)
  between operations  1.29 us (2%)
    pallas_call x1, Pallas kernels, attention(): pl.pallas_call(functools.partial(attention_kernel, n_p, n_b, pair_count),...  49.3 us
    unnamed x7, local copies, waits for them, and re-layouts  8.88 us
    reshape x2, local copies, waits for them, and re-layouts, body(): prefix_kv.reshape(per, 2, pairs, 2, HEAD_SIZE)  1.35 us

profile of v4, /device:TPU:0, one launch (start us, length us, event | category | flops | bytes accessed | tf_op | source)
XLA Modules:
  0.0 62.2 jit_solution(12289354052688945775)
XLA Ops:
  1.3 0.7 %reshape.20 = bf16[4,2,4,2,128]{4,3,2,1,0:T(2,128)(2,1)S(1)} reshape(bf16[4,2,1024]{2,1,0:T(2,128)(2,1)} %param.8) | data formatting | bytes 32768 | tf_op jit(solution)/shard_map/reshape | solution.py:321
  2.0 0.6 copy.10
  2.6 49.3 %attention.1 = (bf16[512,2048]{1,0:T(8,128)(2,1)}, bf16[512,2048]{1,0:T(8,128)(2,1)}, bf16[2,512,1024]{2,1,0:T(8,128)(2,1)}, bf16[4,16,128]{2,1,0:T(8,128)(2,1)}) custom-call(s32[1]{0:T(128)S(6)} %copy.15.lens, s32[1,512]{1,0:T(1,128)} %ends.1, bf16[512,2048]{1,0:T(8,128)(2,1)} %bitcast.14, bf16[512,2048]{1,0:T(8,128)(2,1)} %bitcast.15, ...), custom_call_target="tpu_custom_call" | custom-call | tf_op jit(solution)/shard_map/attention/pallas_call | solution.py:269
  52.0 0.7 %copy.11 = bf16[4,2,4,2,128]{4,3,2,1,0:T(2,128)(2,1)S(1)} copy(bf16[4,2,4,2,128]{4,0,1,3,2:T(4,128)(2,1)} %bitcast.21) | data formatting | bytes 32768 | tf_op jit(solution)/shard_map/transpose | solution.py:325
  52.7 0.6 reshape.23
  53.3 0.0 copy-start.1
  53.3 5.2 %copy.12 = bf16[1,512,2,1024]{3,2,1,0:T(2,128)(2,1)} copy(bf16[1,512,2,1024]{3,1,2,0:T(8,128)(2,1)} %bitcast.19) | data formatting | bytes 4194304
  58.5 0.0 copy-done.1
  58.5 0.0 copy-start
  58.5 1.3 %copy.16 = bf16[1,512,2048]{2,1,0:T(8,128)(2,1)} copy(bf16[1,512,2048]{2,1,0:T(8,128)(2,1)S(1)} %bitcast.18) | data formatting | bytes 4194304
  59.9 1.0 %copy-done = bf16[512,2048]{1,0:T(8,128)(2,1)S(1)} copy-done((bf16[512,2048]{1,0:T(8,128)(2,1)S(1)}, bf16[512,2048]{1,0:T(8,128)(2,1)}, u32[]{:S(2)}) %copy-start) | copy-done | bytes 2097176
  60.9 1.3 %copy.17 = bf16[1,512,2048]{2,1,0:T(8,128)(2,1)} copy(bf16[1,512,2048]{2,1,0:T(8,128)(2,1)S(1)} %bitcast.17) | data formatting | bytes 4194304
Async XLA Ops:
  53.3 5.2 %copy-start.1 = (bf16[512,2048]{1,0:T(8,128)(2,1)S(1)}, bf16[512,2048]{1,0:T(8,128)(2,1)}, u32[]{:S(2)}) copy-start(bf16[512,2048]{1,0:T(8,128)(2,1)} %get-tuple-element.8) | copy-start | bytes 6291460
  58.5 2.3 %copy-start = (bf16[512,2048]{1,0:T(8,128)(2,1)S(1)}, bf16[512,2048]{1,0:T(8,128)(2,1)}, u32[]{:S(2)}) copy-start(bf16[512,2048]{1,0:T(8,128)(2,1)} %get-tuple-element.9) | copy-start | bytes 6291460
